TPU v7x, 128 devices: a whole 4x4x4 slice. The times are simulated.
128 devices in a mesh: subj: 8 (over z, x_lo), vox: 16 (over y, x_hi, core).
Axes of the slice: x: 4 (x_hi: 2, x_lo: 2; x = x_hi * 2 + x_lo), y: 4, z: 4, core: 2. Of those that a mesh axis runs over, the one named last changes fastest.
Arguments:
- features: bfloat16 [16384, 4096], P(('subj', 'vox')), may hold values from -20 to 20
- token_ticks: int32 [16384], replicated, may hold values from 0 to 98303, as said below
- offsets: int32 [8], P('subj'), may hold values from 0 to 63
- run_lengths: int32 [8, 8], P('subj'), may hold values from 1 to 512, 1536 in all within a row
- penalty: float32 [8], P('subj'), may hold values from 0.05 to 0.5
- responses: float32 [8, 1536, 2048], P('subj', None, 'vox'), may hold values from -6 to 6
Outputs:
- weights: bfloat16 [8, 4, 4096, 2048], P('subj', None, 'vox')
Inputs may be any that keep to these rules, and one draw needn't show every extreme that they name: `token_ticks`: token k's tick lies between k * 6 and k * 6 + 5. `run_lengths`: each subject's 8 runs together cover its 1536 TRs in order.
All inputs are finite; a program needn't handle non-finite values.
Results may differ from a plain program's by a relative error of at most 0.023.
The roundings to bfloat16 on the way count: a program that leaves them out, or rounds other values in their place, can miss the bound.
Values may be sent and summed in bfloat16 or wider, within the bound.
No kernel may reach another device: no remote copies, remote signals or barrier semaphores. Data moves between devices by JAX's collectives and lax.ppermute only.
A program may use at most 128 MiB of HBM per device.

v0:
```python
import math

import jax
import jax.numpy as jnp
from jax import lax
from jax.sharding import PartitionSpec as P

DELAYS = 4
TICKS = 64
GAP = 6


def lanczos_block(near_ticks, offset, first_row, row_count):
    tr_rows = first_row + jnp.arange(row_count, dtype=jnp.int32)
    distance = near_ticks[None, :] - (tr_rows[:, None] * TICKS + offset)
    inside = jnp.abs(distance) < 3 * TICKS
    scaled = distance.astype(jnp.float32) / TICKS
    shaped = jnp.sinc(scaled) * jnp.sinc(scaled / 3.0)
    return jnp.where(inside, shaped, jnp.zeros_like(shaped)).astype(jnp.bfloat16)


def delay_stack(interp, lengths, tr_total):
    starts = jnp.cumsum(lengths) - lengths
    tr_steps = jnp.arange(tr_total, dtype=jnp.int32)
    run_first = jnp.max(jnp.where(starts[None, :] <= tr_steps[:, None], starts[None, :], 0), axis=1)
    delayed = []
    for delay_step in range(1, DELAYS + 1):
        moved = jnp.concatenate(
            [jnp.zeros((delay_step, interp.shape[1]), interp.dtype), interp[:-delay_step]], axis=0
        )
        keep_rows = (tr_steps - delay_step >= run_first)[:, None]
        delayed.append(jnp.where(keep_rows, moved, jnp.zeros_like(moved)))
    return jnp.stack(delayed, axis=1)


def body(features, token_ticks, offsets, run_lengths, penalty, responses):
    tok_dev = features.shape[0]
    width = features.shape[1]
    group_count = lax.axis_size("subj")
    vox_count = lax.axis_size("vox")
    slab_width = width // vox_count
    grouped = lax.all_gather(features, "subj", axis=0, tiled=True)
    mixed_rows = lax.all_to_all(grouped, "vox", split_axis=1, concat_axis=0, tiled=True)
    columns = mixed_rows.reshape(vox_count, group_count, tok_dev, slab_width)
    columns = columns.transpose(1, 0, 2, 3).reshape(vox_count * group_count * tok_dev, slab_width)
    token_count = columns.shape[0]
    tr_total = token_count * GAP // TICKS
    row_block = math.gcd(tr_total, 128)
    window = min((row_block + 5) * TICKS // GAP + 3, token_count)
    offset = offsets[0]
    spread = (GAP / TICKS) ** 0.5

    def interp_block(block_index):
        first_row = block_index * row_block
        lowest_tick = first_row * TICKS + offset - 3 * TICKS
        begin_token = jnp.clip((lowest_tick - GAP + 1) // GAP, 0, token_count - window)
        shard_piece = lax.dynamic_slice_in_dim(columns, begin_token, window, 0)
        near_ticks = lax.dynamic_slice_in_dim(token_ticks, begin_token, window, 0)
        weights_table = lanczos_block(near_ticks, offset, first_row, row_block)
        return jnp.dot(weights_table, shard_piece, preferred_element_type=jnp.float32)

    summed = lax.map(interp_block, jnp.arange(tr_total // row_block, dtype=jnp.int32))
    interp = (summed.reshape(tr_total, slab_width) * spread).astype(jnp.bfloat16)
    stacked = delay_stack(interp, run_lengths[0], tr_total).reshape(tr_total, DELAYS * slab_width)
    partial_kernel = lax.dot_general(
        stacked, stacked, (((1,), (1,)), ((), ())), preferred_element_type=jnp.float32
    )
    kernel = lax.psum(partial_kernel, "vox") / (DELAYS * width)
    system = kernel + penalty[0] * jnp.eye(tr_total, dtype=jnp.float32)
    factor = jnp.linalg.cholesky(system)
    forward = lax.linalg.triangular_solve(factor, responses[0], left_side=True, lower=True)
    dual_coef = lax.linalg.triangular_solve(
        factor, forward, left_side=True, lower=True, transpose_a=True
    ).astype(jnp.bfloat16)
    projected = lax.dot_general(
        stacked,
        lax.all_gather(dual_coef, "vox", axis=1, tiled=True),
        (((0,), (0,)), ((), ())),
        preferred_element_type=jnp.float32,
    )
    projected = (projected * (DELAYS * width) ** (-0.5)).astype(jnp.bfloat16)
    return projected.reshape(1, DELAYS, slab_width, projected.shape[1])


def solution(mesh):
    return jax.shard_map(
        body,
        mesh=mesh,
        in_specs=(
            P(("subj", "vox"), None),
            P(),
            P("subj"),
            P("subj", None),
            P("subj"),
            P("subj", None, "vox"),
        ),
        out_specs=P("subj", None, "vox", None),
        check_vma=False,
    )
```

profile of v0, /device:TPU:1, one launch (start us, length us, event | category | flops | bytes accessed | tf_op | source)
XLA Modules:
  0.0 1268.4 jit_solution(4992571521998766877)
XLA Ops:
  8.8 171.4 %all-gather.3.cloned.1.call-done = bf16[1024,4096]{0,1:T(8,128)(2,1)} async-done(((bf16[128,4096]{0,1:T(8,128)(2,1)}), bf16[1024,4096]{0,1:T(8,128)(2,1)}) %all-gather.3.cloned.1.call-update) | async-done | bytes 8388624 | tf_op jit(solution)/shard_map/all_gather | solution.py:42
  180.2 7.1 all-to-all-start
  187.7 95.7 %all-to-all-done = bf16[1024,16,256]{0,2,1:T(8,128)(2,1)} async-done(((bf16[1024,16,256]{0,2,1:T(8,128)(2,1)}), bf16[1024,16,256]{0,2,1:T(8,128)(2,1)}, u32[]{:S(2)}, u32[]{:S(2)}) %all-to-all-start) | async-done | bytes 8388640 | tf_op jit(solution)/shard_map/all_to_all | solution.py:43
  283.4 12.3 copy.91
  295.6 7.7 copy.92
  303.4 86.4 %while.15 = (s32[]{:T(128)}, f32[12,128,256]{2,1,0:T(8,128)S(1)}, s32[12]{0:T(128)S(1)}, s32[]{:T(128)}, s32[16384]{0:T(1024)}, /*index=5*/bf16[16384,256]{1,0:T...) while((s32[]{:T(128)}, f32[12,128,256]{2,1,0:T(8,128)S(1)}, ...), condition=%wide.region_3.5_spmd, body=%wide.region_2.4_spmd.sunk | while | flops 106768656 | bytes 881067 | solution.py:62
  307.2 3.4 fusion.283
  314.4 3.4 fusion.283
  321.6 3.4 fusion.283
  328.8 3.4 fusion.283
  336.0 3.4 fusion.283
  343.2 3.4 fusion.283
  350.4 3.4 fusion.283
  357.6 3.4 fusion.283
  364.8 3.4 fusion.283
  372.0 3.4 fusion.283
  379.2 3.4 fusion.283
  386.4 3.4 fusion.283
  393.6 8.8 convolution_bitcast_fusion.1
  403.2 213.6 %all-reduce.7.cloned.1.call-done = f32[1536,1536]{0,1:T(8,128)} async-done(((f32[1536,1536]{0,1:T(8,128)}), f32[1536,1536]{0,1:T(8,128)}) %all-reduce.7.cloned.1.call-update) | async-done | bytes 9437200 | tf_op jit(solution)/shard_map/psum | solution.py:68
  616.8 8.5 select_add_fusion
  625.3 9.9 copy.95
  635.2 12.6 fusion.78
  648.6 11.7 cholesky.340
  660.5 9.8 custom-call.96
  674.3 12.1 cholesky.361
  686.5 9.8 custom-call.97
  698.3 3.6 copy-done
  702.0 3.3 convolution_subtract_fusion.1
  705.3 11.7 cholesky.384
  717.8 9.9 custom-call.98
  729.3 4.7 convolution_subtract_fusion
  734.0 11.7 cholesky.713
  746.5 9.8 custom-call.99
  757.8 5.4 fusion.95
  763.2 11.7 cholesky.732
  775.7 9.8 custom-call.100
  786.9 6.0 fusion.98
  793.0 11.7 cholesky.752
  805.5 9.8 custom-call.101
  816.6 5.7 fusion.101
  822.2 11.9 cholesky.772
  834.9 9.8 custom-call.102
  845.9 5.6 fusion.104
  851.6 11.9 cholesky.792
  864.2 9.8 custom-call.103
  875.2 5.2 fusion.107
  880.4 11.7 cholesky.812
  892.9 10.2 custom-call.104
  904.2 4.7 fusion.110
  908.9 11.7 cholesky.832
  921.4 9.8 custom-call.105
  932.3 3.9 fusion.113
  936.2 11.7 cholesky.852
  948.7 9.8 custom-call.106
  959.4 2.7 convolution_subtract_fusion.5
  962.2 11.7 cholesky.870
  990.6 8.6 select_select_fusion
  999.2 37.1 %while.16 = (s32[]{:T(128)}, f32[1536,1536]{0,1:T(8,128)}, s32[12,2]{0,1:T(2,128)S(1)}, f32[12,128,128]{2,1,0:T(8,128)S(1)}, s32[]{:T(128)}) while((s32[]{:T(128)}, f32[1536,1536]{0,1:T(8,128)}, s32[12,2]{0,1:T(2,128)S(1)}, f32[12,128,128]{2,1,0:T(8,128)S(1)}, s32[]{:T(128)}) %tuple.136), condition=%wide.while_cond, body=%wide.while_body.sunk | while | flops 2 | bytes 393329 | solution.py:72
  1003.0 2.3 dynamic-slice.7
  1036.3 117.9 %custom-call.107 = f32[12,128,128]{1,2,0:T(8,128)S(1)} custom-call(f32[12,128,128]{2,1,0:T(8,128)S(1)} %get-tuple-element.141), custom_call_target="InvertDiagBlocksLowerTriangular" | custom-call | tf_op jit(solution)/shard_map/triangular_solve | solution.py:72
  1186.3 2.9 copy.93
  1189.2 61.5 %all-gather.5.cloned.1.call-done = bf16[1536,2048]{1,0:T(8,128)(2,1)} async-done(((bf16[1536,128]{1,0:T(8,128)(2,1)}), bf16[1536,2048]{1,0:T(8,128)(2,1)}) %all-gather.5.cloned.1.call-update) | async-done | bytes 6291472 | tf_op jit(solution)/shard_map/all_gather | solution.py:77
  1250.7 11.0 multiply_convert_fusion
  (311 shorter events, 130.9 us)
Async XLA Ops:
  6.5 173.7 %all-gather.3.cloned.1.call-start = ((), (), s32[]{:S(2)}) async-start(), calls=%async_computation.1 | async-start | bytes 9437184 | tf_op jit(solution)/shard_map/all_gather | solution.py:42
  8.8 178.6 %copy-start.8 = (s32[1,8]{1,0:T(1,128)S(1)}, s32[1,8]{1,0:T(1,128)}, u32[]{:S(2)}) copy-start(s32[1,8]{1,0:T(1,128)} %param.12) | copy-start | bytes 100
  180.2 103.1 %all-to-all-start = ((bf16[1024,16,256]{0,2,1:T(8,128)(2,1)}), bf16[1024,16,256]{0,2,1:T(8,128)(2,1)}, u32[]{:S(2)}, u32[]{:S(2)}) async-start(bf16[1024,16,256]{0,2,1:T(8,128)(2,1)} %bitcast.269), calls=%async_computation | async-start | bytes 16777216 | tf_op jit(solution)/shard_map/all_to_all | solution.py:43
  187.3 429.5 %all-reduce.7.cloned.1.call-start = ((), (), s32[]{:S(2)}) async-start(), calls=%async_computation.2 | async-start | bytes 18874368 | tf_op jit(solution)/shard_map/psum | solution.py:68
  391.2 1.2 copy-start.2
  391.2 1.2 copy-start.3
  392.4 0.9 copy-start.4
  392.4 1.2 copy-start.5
  402.5 848.2 %all-gather.5.cloned.1.call-start = ((), (), s32[]{:S(2)}) async-start(), calls=%async_computation.3 | async-start | bytes 6684672 | tf_op jit(solution)/shard_map/all_gather | solution.py:77
  698.3 3.7 copy-start
  990.6 163.6 %copy-start.6 = (f32[1,1536,128]{2,1,0:T(8,128)S(1)}, f32[1,1536,128]{2,1,0:T(8,128)}, u32[]{:S(2)}) copy-start(f32[1,1536,128]{2,1,0:T(8,128)} %param.14) | copy-start | bytes 2359300
  1154.2 13.9 %copy-start.1 = (f32[1536,1536]{0,1:T(8,128)S(1)}, f32[1536,1536]{0,1:T(8,128)}, u32[]{:S(2)}) copy-start(f32[1536,1536]{0,1:T(8,128)} %get-tuple-element.420) | copy-start | bytes 28311556
  1183.4 0.7 copy-start.7
Sparse Core Ops, SparseCore 0:
  8.9 171.2 all-gather.2
  402.6 214.1 all-reduce.6
  1184.3 66.3 all-gather.4
where the time goes:
time: 1280 us; the launch traced here: 1270 us
  waiting for transfers between devices  542 us (42%)
  other arithmetic  419 us (33%)
  matrix products  151 us (12%)
  local copies, waits for them, and re-layouts  104 us (8%)
  between operations  22.8 us (2%)
  loops' own time  22.3 us (2%)
    another operation x47, other arithmetic, body(): factor = jnp.linalg.cholesky(system)  258 us
    psum x1, waiting for transfers between devices, body(): kernel = lax.psum(partial_kernel, 'vox') / (DELAYS * width)  214 us
    all_gather x1, waiting for transfers between devices, body(): grouped = lax.all_gather(features, 'subj', axis=0, tiled=True)  171 us
    another operation x4, other arithmetic, body(): lax.linalg.triangular_solve(factor, forward, left_side=True, lower=True,...  126 us
    all_to_all x1, waiting for transfers between devices, body(): lax.all_to_all(grouped, 'vox', split_axis=1, concat_axis=0, tiled=True)  95.7 us
    another operation x22, matrix products, body(): factor = jnp.linalg.cholesky(system)  62.8 us
    all_gather x1, waiting for transfers between devices, body(): lax.all_gather(dual_coef, 'vox', axis=1, tiled=True)  61.5 us
    dot_general x12, matrix products, interp_block(): jnp.dot(weights_table, shard_piece, preferred_element_type=jnp.float32)  40.3 us
  transfers between devices with their start and end apart: 4, of which 4 were waited for; matrix products, arithmetic and copies ran while one was open for 0% of the time, Pallas kernels for 0%

commit v1 on v0

v1 whole, which is shorter than its diff:
```python
import jax
import jax.numpy as jnp
from jax import lax
from jax.experimental import pallas as pl
from jax.experimental.pallas import tpu as pltpu
from jax.sharding import PartitionSpec as P

DELAYS = 4
TICKS = 64
GAP = 6
F = 4096
SUBJ = 8
VOX = 16
N = 1536
SLAB = F // VOX
COLS = 128
W = 256
PANELS = N // W
EDGE = 16
HALO = 32
STEP = 24
HI = lax.Precision.HIGHEST
NT = (((1,), (1,)), ((), ()))


def mm(a, b):
    return jnp.dot(a, b, precision=HI, preferred_element_type=jnp.float32)


def mmt(a, b):
    return lax.dot_general(a, b, NT, precision=HI, preferred_element_type=jnp.float32)


def tri_inverse(block):
    rows = [block[8 * g : 8 * g + 8, :] for g in range(16)]
    shape = (8, 128)
    lane = lax.broadcasted_iota(jnp.int32, shape, 1)
    sub = lax.broadcasted_iota(jnp.int32, shape, 0)
    for g in range(16):
        base = 8 * g
        here = rows[g]
        col = [jnp.broadcast_to(here[:, base + m : base + m + 1], shape) for m in range(8)]
        a = [[jnp.broadcast_to(col[m][j : j + 1, :], shape) for m in range(j + 1)] for j in range(8)]
        x = [[None] * 8 for _ in range(8)]
        for p in range(8):
            inv = lax.rsqrt(a[p][p])
            for j in range(p):
                x[p][j] = x[p][j] * inv
            x[p][p] = inv
            low = {i: a[i][p] * inv for i in range(p + 1, 8)}
            for i in range(p + 1, 8):
                for j in range(p + 1, i + 1):
                    a[i][j] = a[i][j] - low[i] * low[j]
                for j in range(p + 1):
                    term = low[i] * x[p][j]
                    x[i][j] = -term if x[i][j] is None else x[i][j] - term
        inside = (lane >= base) & (lane < base + 8)
        unit = jnp.where(inside, jnp.where(lane - base == sub, 1.0, 0.0), here)
        r = [jnp.broadcast_to(unit[m : m + 1, :], shape) for m in range(8)]
        hat = []
        for q in range(8):
            acc = x[q][0] * r[0]
            for m in range(1, q + 1):
                acc = acc + x[q][m] * r[m]
            hat.append(acc)
        out = hat[0]
        for q in range(1, 8):
            out = jnp.where(sub == q, hat[q], out)
        rows[g] = jnp.where(lane < base + 8, out, 0.0)
        if g < 15:
            full = []
            for m in range(8):
                acc = x[7][m] * hat[7]
                for q in range(6, m - 1, -1):
                    acc = acc + x[q][m] * hat[q]
                full.append(acc)
            for i in range(g + 1, 16):
                old = rows[i]
                acc = jnp.where(inside, 0.0, old)
                for m in range(8):
                    acc = acc - jnp.broadcast_to(old[:, base + m : base + m + 1], shape) * full[m]
                rows[i] = acc
    return jnp.concatenate(rows, axis=0)


def cut(i, size=W):
    return pl.ds(pl.multiple_of(i * size, size), size)


def solve_kernel(pen_ref, all_ref, b_ref, pr_ref, pc_ref, o_ref, xs_ref, a_ref, strip_ref, inv_ref, sem):
    tail = pl.ds(N, COLS)
    copies = [
        pltpu.make_async_copy(all_ref.at[v], xs_ref.at[pl.ds(EDGE, N), pl.ds(v * SLAB, SLAB)], sem.at[v])
        for v in range(VOX)
    ]
    copies.append(pltpu.make_async_copy(b_ref, a_ref.at[tail, :], sem.at[VOX]))
    for c in copies:
        c.start()
    xs_ref[0:EDGE, :] = jnp.zeros((EDGE, F), jnp.bfloat16)
    strip_ref[:, 0:128] = jnp.zeros((W + EDGE, 128), jnp.float32)
    for c in copies:
        c.wait()
    pen = pen_ref[0]
    scale = 1.0 / (DELAYS * F)

    def gram(i, _):
        left = xs_ref[pl.ds(pl.multiple_of(i * W, W), W + EDGE), :]

        def one(j, _):
            right = xs_ref[pl.ds(pl.multiple_of(j * W + EDGE, EDGE), W), :]
            strip_ref[:, pl.ds(pl.multiple_of(j * W + 128, 128), W)] = lax.dot_general(
                left, right, NT, preferred_element_type=jnp.float32
            )
            return 0

        lax.fori_loop(0, i + 1, one, 0)
        row_pos = pr_ref[cut(i), :]

        def shift(j, _):
            t = strip_ref[:, pl.ds(pl.multiple_of(j * W, 128), W + 128)]
            near = jnp.minimum(row_pos, pc_ref[0:1, cut(j)])
            total = jnp.zeros((W, W), jnp.float32)
            for k in range(1, DELAYS + 1):
                t = pltpu.roll(pltpu.roll(t, 1, 0), 1, 1)
                total = total + jnp.where(near >= k, t[EDGE:, 128:], 0.0)
            total = total * scale
            row = lax.broadcasted_iota(jnp.int32, (W, W), 0) + i * W
            colm = lax.broadcasted_iota(jnp.int32, (W, W), 1) + j * W
            a_ref[cut(i), cut(j)] = jnp.where(row == colm, total + pen, total)
            return 0

        lax.fori_loop(0, i + 1, shift, 0)
        return 0

    lax.fori_loop(0, PANELS, gram, 0)

    def panel(p, _):
        def half(h, _):
            d = 2 * p + h
            blk = cut(d, 128)
            inv_ref[p, cut(h, 128), cut(h, 128)] = tri_inverse(a_ref[blk, blk])

            @pl.when(h == 0)
            def _():
                below = cut(d + 1, 128)
                c = mmt(a_ref[below, blk], inv_ref[p, 0:128, 0:128])
                a_ref[below, blk] = c
                a_ref[below, below] -= mmt(c, c)

            return 0

        lax.fori_loop(0, 2, half, 0)
        low = a_ref[cut(2 * p + 1, 128), cut(2 * p, 128)]
        inv_ref[p, 128:256, 0:128] = -mm(inv_ref[p, 128:256, 128:256], mm(low, inv_ref[p, 0:128, 0:128]))
        inv_ref[p, 0:128, 128:256] = jnp.zeros((128, 128), jnp.float32)
        here = cut(p)

        def scale_rows(i, _):
            a_ref[cut(i), here] = mmt(a_ref[cut(i), here], inv_ref[p])
            return 0

        lax.fori_loop(p + 1, PANELS, scale_rows, 0)
        a_ref[tail, here] = mmt(a_ref[tail, here], inv_ref[p])

        def column(j, _):
            right = a_ref[cut(j), here]

            def update(i, _):
                a_ref[cut(i), cut(j)] -= mmt(a_ref[cut(i), here], right)
                return 0

            lax.fori_loop(j, PANELS, update, 0)
            a_ref[tail, cut(j)] -= mmt(a_ref[tail, here], right)
            return 0

        lax.fori_loop(p + 1, PANELS, column, 0)
        return 0

    lax.fori_loop(0, PANELS, panel, 0)

    def back(q, _):
        p = PANELS - 1 - q
        x = mm(a_ref[tail, cut(p)], inv_ref[p])
        a_ref[tail, cut(p)] = x

        def push(j, _):
            a_ref[tail, cut(j)] -= mm(x, a_ref[cut(p), cut(j)])
            return 0

        lax.fori_loop(0, p, push, 0)
        return 0

    lax.fori_loop(0, PANELS, back, 0)
    o_ref[...] = a_ref[tail, :].astype(o_ref.dtype)


def solve_call(pen, gathered, targets, row_pos, col_pos):
    anywhere = pl.BlockSpec(memory_space=pl.ANY)
    vmem = pl.BlockSpec(memory_space=pltpu.VMEM)
    return pl.pallas_call(
        solve_kernel,
        out_shape=jax.ShapeDtypeStruct((COLS, N), jnp.bfloat16),
        in_specs=[pl.BlockSpec(memory_space=pltpu.SMEM), anywhere, anywhere, vmem, vmem],
        out_specs=vmem,
        scratch_shapes=[
            pltpu.VMEM((N + EDGE, F), jnp.bfloat16),
            pltpu.VMEM((N + COLS, N), jnp.float32),
            pltpu.VMEM((W + EDGE, N + 128), jnp.float32),
            pltpu.VMEM((PANELS, W, W), jnp.float32),
            pltpu.SemaphoreType.DMA((VOX + 1,)),
        ],
        compiler_params=pltpu.CompilerParams(vmem_limit_bytes=52 * 2**20),
        cost_estimate=pl.CostEstimate(flops=3 * 10**10, bytes_accessed=2 * 10**7, transcendentals=0),
    )(pen, gathered, targets, row_pos, col_pos)


def lanczos(ticks, centers):
    distance = ticks[None, :] - centers[:, None]
    inside = jnp.abs(distance) < 3 * TICKS
    scaled = distance.astype(jnp.float32) / TICKS
    shaped = jnp.sinc(scaled) * jnp.sinc(scaled / 3.0)
    return jnp.where(inside, shaped, jnp.zeros_like(shaped)).astype(jnp.bfloat16)


def all_offsets(offsets):
    mine = lax.axis_index("subj")
    wide = jnp.broadcast_to(offsets, (8, 128))
    got = [wide]
    for hop in range(1, SUBJ):
        got.append(lax.ppermute(wide, "subj", [(i, (i - hop) % SUBJ) for i in range(SUBJ)]))
    stacked = jnp.stack([g[0, 0] for g in got])
    return jnp.roll(stacked, mine)


def body(features, token_ticks, offsets, run_lengths, penalty, responses):
    group = lax.axis_index("subj")
    rows = N // SUBJ
    tokens = token_ticks.shape[0] // SUBJ
    every = all_offsets(offsets)
    columns = lax.all_to_all(features, "vox", split_axis=1, concat_axis=0, tiled=True)
    before = lax.ppermute(columns[-HALO:], "subj", [(i, i + 1) for i in range(SUBJ - 1)])
    after = lax.ppermute(columns[:HALO], "subj", [(i + 1, i) for i in range(SUBJ - 1)])
    ext = jnp.concatenate([before, columns, after], axis=0)
    far = jnp.full((HALO,), -(2**20), jnp.int32)
    near_ticks = lax.dynamic_slice_in_dim(
        jnp.concatenate([far, token_ticks, far]), group * tokens, tokens + 2 * HALO, 0
    )
    spread = (GAP / TICKS) ** 0.5
    span = STEP * TICKS // GAP
    steps = jnp.arange(STEP, dtype=jnp.int32)
    pieces = []
    for b in range(rows // STEP):
        first = group * rows + b * STEP
        centers = ((first + steps)[None, :] * TICKS + every[:, None]).reshape(-1)
        low = b * span
        table = lanczos(near_ticks[low : low + span + 2 * HALO], centers)
        summed = jnp.dot(table, ext[low : low + span + 2 * HALO], preferred_element_type=jnp.float32)
        pieces.append((summed * spread).astype(jnp.bfloat16).reshape(SUBJ, STEP, SLAB))
    local = jnp.stack(pieces, axis=1).reshape(SUBJ * rows, SLAB)
    interp = lax.all_to_all(local, "subj", split_axis=0, concat_axis=0, tiled=True)
    gathered = lax.all_gather(interp, "vox", axis=0, tiled=False)

    lengths = run_lengths[0]
    starts = jnp.cumsum(lengths) - lengths
    tr_steps = jnp.arange(N, dtype=jnp.int32)
    run_first = jnp.max(jnp.where(starts[None, :] <= tr_steps[:, None], starts[None, :], 0), axis=1)
    pos = tr_steps - run_first
    dual = solve_call(
        penalty,
        gathered,
        responses[0].T,
        pos[:, None],
        jnp.broadcast_to(pos[None, :], (8, N)),
    )
    delayed = []
    for k in range(1, DELAYS + 1):
        moved = jnp.concatenate([jnp.zeros((k, SLAB), interp.dtype), interp[:-k]], axis=0)
        delayed.append(jnp.where((pos >= k)[:, None], moved, jnp.zeros_like(moved)))
    stacked = jnp.concatenate(delayed, axis=1)
    projected = lax.dot_general(
        stacked,
        lax.all_gather(dual, "vox", axis=0, tiled=True),
        (((0,), (1,)), ((), ())),
        preferred_element_type=jnp.float32,
    )
    projected = (projected * (DELAYS * F) ** (-0.5)).astype(jnp.bfloat16)
    return projected.reshape(1, DELAYS, SLAB, projected.shape[1])


def solution(mesh):
    return jax.shard_map(
        body,
        mesh=mesh,
        in_specs=(
            P(("subj", "vox"), None),
            P(),
            P("subj"),
            P("subj", None),
            P("subj"),
            P("subj", None, "vox"),
        ),
        out_specs=P("subj", None, "vox", None),
        check_vma=False,
    )
```

time: 1280 us -> 384 us (0.30)
  other arithmetic: 419 us -> 3.02 us
  waiting for transfers between devices: 542 us -> 157 us
  Pallas kernels: 0 us -> 134 us
  matrix products: 151 us -> 18.3 us
  local copies, waits for them, and re-layouts: 104 us -> 18 us
  loops' own time: 22.3 us -> 0 us
  starting transfers between devices: 7.18 us -> 24.7 us
  blocking collectives: 0 us -> 13.9 us
    another operation x55 -> x1, other arithmetic: 390 us -> 0.18 us  [the longest x47 258 us: body(): factor = jnp.linalg.cholesky(system)]
    psum x1 -> x0, waiting for transfers between devices: 214 us -> none  [body(): kernel = lax.psum(partial_kernel, 'vox') / (DELAYS * width)]
    pallas_call x0 -> x1, Pallas kernels: none -> 134 us  [solve_call(): pl.pallas_call(solve_kernel, out_shape=jax.ShapeDtypeStruct((COLS, N), jn...]
    all_to_all x1, waiting for transfers between devices: 95.7 us -> 0.01 us  [body(): lax.all_to_all(features, 'vox', split_axis=1, concat_axis=0, tiled=True)]
    another operation x68 -> x0, matrix products: 90.7 us -> none  [the longest x22 62.8 us: body(): factor = jnp.linalg.cholesky(system)]
    all_gather x2, waiting for transfers between devices: 233 us -> 151 us  [the longest x1 91.8 us: body(): gathered = lax.all_gather(interp, 'vox', axis=0, tiled=False)]
    another operation x106 -> x1, local copies, waits for them, and re-layouts: 49.7 us -> 0.05 us  [body(): local = jnp.stack(pieces, axis=1).reshape(SUBJ * rows, SLAB)]
    dot_general x14 -> x9, matrix products: 60.1 us -> 18.3 us  [the longest x1 10.4 us: body(): lax.dot_general(stacked, lax.all_gather(dual, 'vox', axis=0, tiled=True),...]
  transfers between devices with their start and end apart: 4 -> 12, of which waited for: 4 -> 3; matrix products, arithmetic and copies ran while one was open for 0% -> 7% of each run, Pallas kernels for 0% -> 0%
where the time goes in v1:
time: 384 us; the launch traced here: 383 us
  waiting for transfers between devices  157 us (41%)
  Pallas kernels  134 us (35%)
  starting transfers between devices  24.7 us (6%)
  matrix products  18.3 us (5%)
  local copies, waits for them, and re-layouts  18 us (5%)
  between operations  15 us (4%)
  blocking collectives  13.9 us (4%)
    pallas_call x1, Pallas kernels, solve_call(): pl.pallas_call(solve_kernel, out_shape=jax.ShapeDtypeStruct((COLS, N), jn...  134 us
    all_gather x1, waiting for transfers between devices, body(): gathered = lax.all_gather(interp, 'vox', axis=0, tiled=False)  91.8 us
    all_gather x1, waiting for transfers between devices, body(): lax.all_gather(dual, 'vox', axis=0, tiled=True)  59.5 us
    all_to_all x1, blocking collectives, body(): lax.all_to_all(local, 'subj', split_axis=0, concat_axis=0, tiled=True)  13.9 us
    ppermute x7, starting transfers between devices, all_offsets(): lax.ppermute(wide, 'subj', [(i, (i - hop) % SUBJ) for i in range(SUBJ)])  10.7 us
    dot_general x1, matrix products, body(): lax.dot_general(stacked, lax.all_gather(dual, 'vox', axis=0, tiled=True),...  10.4 us
    concatenate x1, local copies, waits for them, and re-layouts, all_offsets(): return jnp.roll(stacked, mine)  9.07 us
    all_to_all x1, starting transfers between devices, body(): lax.all_to_all(features, 'vox', split_axis=1, concat_axis=0, tiled=True)  8.45 us
  transfers between devices with their start and end apart: 12, of which 3 were waited for; matrix products, arithmetic and copies ran while one was open for 7% of the time, Pallas kernels for 0%

profile of v1, /device:TPU:1, one launch (start us, length us, event | category | flops | bytes accessed | tf_op | source)
XLA Modules:
  0.0 383.4 jit_solution(11873622523696685469)
XLA Ops:
  6.5 2.3 copy.33
  8.8 8.4 %all-to-all-start = ((bf16[128,16,256]{0,2,1:T(8,128)(2,1)}), bf16[128,16,256]{0,2,1:T(8,128)(2,1)S(1)}, u32[]{:S(2)}, u32[]{:S(2)}) async-start(bf16[128,16,256]{0,2,1:T(8,128)(2,1)} %bitcast.9), calls=%async_computation | async-start | bytes 2097152 | tf_op jit(solution)/shard_map/all_to_all | solution.py:240
  17.2 0.0 all-gather.3.cloned.1.call-start
  17.9 0.4 collective-permute-start.6
  18.3 1.6 collective-permute-start.5
  20.0 3.6 collective-permute-start.4
  23.6 0.9 collective-permute-start.3
  24.4 2.7 collective-permute-start.2
  27.2 0.9 concatenate.30
  28.1 0.1 fusion.627
  28.3 5.3 %collective-permute-done.6 = s32[8,128]{1,0:T(8,128)S(1)} collective-permute-done((s32[8,128]{1,0:T(8,128)S(1)}, s32[8,128]{1,0:T(8,128)S(1)}, u32[]{:S(2)}, u32[]{:S(2)}) %collective-permute-start.6) | collective-permute-done | bytes 4128 | tf_op jit(solution)/shard_map/ppermute | solution.py:230
  33.6 0.1 collective-permute-start.1
  33.7 1.3 collective-permute-start
  35.1 0.5 slice.97
  35.6 0.6 slice.96
  36.2 0.6 slice.95
  36.8 0.0 collective-permute-done.3
  36.8 0.5 slice.94
  37.3 0.0 collective-permute-done.2
  37.3 0.6 slice.93
  37.9 0.5 slice.92
  38.4 0.0 collective-permute-done
  38.4 0.6 slice.91
  39.0 9.1 %concatenate.31 = s32[16]{0:T(128)S(1)} concatenate(s32[1]{0:T(128)} %copy.52, s32[1]{0:T(128)} %bitcast.2, s32[1]{0:T(128)} %bitcast.3, s32[1]{0:T(128)} %bitcast.4, s32[1]{0:T(128)} %bitcast.5, s32[1]{0:T(128)} %bitcast.6, s32[1]{0:T(128)} %bitcast.7, s32[1]{0:T(128)} %bitcast.8, s32[1]{0:T(128)} %copy.52, s32[1]{0:T(128)} %bitcast.2, s32[1]{0:T(128)} %bitcast.3, s32[1]{0:T(128)} %bitcast.4, ...), dimensions={0} | concatenate | bytes 128 | tf_op jit(solution)/shard_map/jit(_roll_dynamic)/concatenate | solution.py:232
  48.1 0.1 dynamic_slice.8
  48.2 0.1 broadcast_add_fusion
  48.2 0.1 add.357
  48.3 0.1 add.321
  48.4 0.1 add.327
  48.5 0.1 add.333
  48.5 0.1 add.339
  48.6 0.1 add.345
  48.7 0.1 add.351
  48.8 0.1 add.315
  48.9 0.0 all-to-all-done
  48.9 0.5 copy.34
  49.4 1.3 collective-permute-start.8
  50.7 4.0 %collective-permute-start.7 = (bf16[32,256]{1,0:T(8,128)(2,1)S(1)}, bf16[32,256]{1,0:T(8,128)(2,1)S(1)}, u32[]{:S(2)}, u32[]{:S(2)}) collective-permute-start(bf16[32,256]{1,0:T(8,128)(2,1)S(1)} %get-tuple-element.7), channel_id=1, source_target_pairs={{0,16},{16,32},{32,48},{48,64},{64,80},{80,96},{96,112},{1,17},{17... | collective-permute-start | bytes 49160 | tf_op jit(solution)/shard_map/ppermute | solution.py:241
  54.7 1.0 fusion.13
  55.7 1.0 fusion.12
  56.7 1.0 fusion.11
  57.7 1.0 fusion.10
  58.7 1.0 fusion.9
  59.7 1.0 fusion.8
  60.7 0.0 collective-permute-done.7
  60.7 1.0 fusion.7
  61.7 0.0 copy-start.1
  61.9 1.0 fusion.14
  62.9 13.9 %all_to_all.31 = bf16[8,192,256]{2,1,0:T(8,128)(2,1)} all-to-all(bf16[8,192,256]{2,1,0:T(8,128)(2,1)S(1)} %bitcast.66), channel_id=1, replica_groups=mesh['subj'=8,'vox'=16] {'subj'}, dimensions={0} | all-to-all | bytes 1572864 | tf_op jit(solution)/shard_map/all_to_all | solution.py:260
  76.8 0.0 all-gather.3.cloned.1.call-update
  76.8 0.2 all-gather.5.cloned.1.call-start
  77.7 0.2 reduce-window_clone.1
  77.9 0.3 copy.43
  78.2 0.1 select_reduce_fusion
  78.3 0.3 reshape_subtract_fusion.pr_ref
  78.5 91.8 %all-gather.3.cloned.1.call-done.all_ref = bf16[16,1536,256]{2,1,0:T(8,128)(2,1)} async-done(((bf16[1,1536,256]{2,1,0:T(8,128)(2,1)}), bf16[16,1536,256]{2,1,0:T(8,128)(2,1)}) %all-gather.3.cloned.1.call-update) | async-done | bytes 12582928 | tf_op jit(solution)/shard_map/all_gather | solution.py:261
  170.3 133.9 %shard_map.67 = bf16[128,1536]{1,0:T(8,128)(2,1)} custom-call(f32[1]{0:T(128)S(6)} %copy.53.pen_ref, bf16[16,1536,256]{2,1,0:T(8,128)(2,1)} %all-gather.3.cloned.1.call-done.all_ref, f32[128,1536]{1,0:T(8,128)S(1)} %bitcast.50, s32[1536,1]{1,0:T(8,128)S(1)} %reshape_subtract_fusion.pr_ref, s32[8,1536]{1,0:T(8,128)S(1)} %broadcast_in_dim.46.pc_ref), custom_call_target="tpu_custom_call" | custom-call | flops 30000001024 | bytes 20000000 | tf_op jit(solution)/shard_map/pallas_call | solution.py:200
  304.2 0.0 all-gather.5.cloned.1.call-update
  304.3 0.4 pad_select_fusion.3
  304.7 0.4 pad_select_fusion.2
  305.0 0.4 pad_select_fusion.1
  305.4 1.3 pad_select_fusion
  306.7 59.5 %all-gather.5.cloned.1.call-done = bf16[2048,1536]{1,0:T(8,128)(2,1)} async-done(((bf16[128,1536]{1,0:T(8,128)(2,1)}), bf16[2048,1536]{1,0:T(8,128)(2,1)}) %all-gather.5.cloned.1.call-update) | async-done | bytes 6291472 | tf_op jit(solution)/shard_map/all_gather | solution.py:282
  366.2 10.4 %multiply_convert_fusion = bf16[1024,2048]{1,0:T(8,128)(2,1)} fusion(bf16[2048,1536]{1,0:T(8,128)(2,1)} %all-gather.5.cloned.1.call-done, bf16[1536,256]{1,0:T(8,128)(2,1)} %pad_select_fusion, bf16[1536,256]{1,0:T(8,128)(2,1)S(1)} %pad_select_fusion.1, bf16[1536,256]{1,0:T(8,128)(2,1)S(1)} %pad_select_fusion.2, bf16[1536,256]{1,0:T(8,128)(2,1)S(1)} %pad_select_fusion.3), kind=kOutput, calls=%fused_computation | convolution fusion | flops 6459228160 | bytes 13631488 | tf_op jit(solution)/shard_map/dot_general | solution.py:280
  (28 shorter events, 0.2 us)
Async XLA Ops:
  8.8 40.1 %all-to-all-start = ((bf16[128,16,256]{0,2,1:T(8,128)(2,1)}), bf16[128,16,256]{0,2,1:T(8,128)(2,1)S(1)}, u32[]{:S(2)}, u32[]{:S(2)}) async-start(bf16[128,16,256]{0,2,1:T(8,128)(2,1)} %bitcast.9), calls=%async_computation | async-start | bytes 2097152 | tf_op jit(solution)/shard_map/all_to_all | solution.py:240
  17.2 153.1 %all-gather.3.cloned.1.call-start = ((), (), s32[]{:S(2)}) async-start(), calls=%async_computation.2 | async-start | bytes 13369344 | tf_op jit(solution)/shard_map/all_gather | solution.py:261
  17.9 15.7 %collective-permute-start.6 = (s32[8,128]{1,0:T(8,128)S(1)}, s32[8,128]{1,0:T(8,128)S(1)}, u32[]{:S(2)}, u32[]{:S(2)}) collective-permute-start(s32[8,128]{1,0:T(8,128)S(1)} %broadcast_in_dim.38), channel_id=1, source_target_pairs={{0,16},{16,32},{32,48},{48,64},{64,80},{80,96},{96,112},{112,0},{1... | collective-permute-start | bytes 12296 | tf_op jit(solution)/shard_map/ppermute | solution.py:230
  18.3 15.4 %collective-permute-start.5 = (s32[8,128]{1,0:T(8,128)S(1)}, s32[8,128]{1,0:T(8,128)S(1)}, u32[]{:S(2)}, u32[]{:S(2)}) collective-permute-start(s32[8,128]{1,0:T(8,128)S(1)} %broadcast_in_dim.38), channel_id=1, source_target_pairs={{0,32},{16,48},{32,64},{48,80},{64,96},{80,112},{96,0},{112,16},{1... | collective-permute-start | bytes 12296 | tf_op jit(solution)/shard_map/ppermute | solution.py:230
  20.0 16.2 %collective-permute-start.4 = (s32[8,128]{1,0:T(8,128)S(1)}, s32[8,128]{1,0:T(8,128)S(1)}, u32[]{:S(2)}, u32[]{:S(2)}) collective-permute-start(s32[8,128]{1,0:T(8,128)S(1)} %broadcast_in_dim.38), channel_id=1, source_target_pairs={{0,48},{16,64},{32,80},{48,96},{64,112},{80,0},{96,16},{112,32},{1... | collective-permute-start | bytes 12296 | tf_op jit(solution)/shard_map/ppermute | solution.py:230
  23.6 13.2 %collective-permute-start.3 = (s32[8,128]{1,0:T(8,128)S(1)}, s32[8,128]{1,0:T(8,128)S(1)}, u32[]{:S(2)}, u32[]{:S(2)}) collective-permute-start(s32[8,128]{1,0:T(8,128)S(1)} %broadcast_in_dim.38), channel_id=1, source_target_pairs={{0,64},{16,80},{32,96},{48,112},{64,0},{80,16},{96,32},{112,48},{1... | collective-permute-start | bytes 12296 | tf_op jit(solution)/shard_map/ppermute | solution.py:230
  24.4 12.9 %collective-permute-start.2 = (s32[8,128]{1,0:T(8,128)S(1)}, s32[8,128]{1,0:T(8,128)S(1)}, u32[]{:S(2)}, u32[]{:S(2)}) collective-permute-start(s32[8,128]{1,0:T(8,128)S(1)} %broadcast_in_dim.38), channel_id=1, source_target_pairs={{0,80},{16,96},{32,112},{48,0},{64,16},{80,32},{96,48},{112,64},{1... | collective-permute-start | bytes 12296 | tf_op jit(solution)/shard_map/ppermute | solution.py:230
  33.6 4.3 %collective-permute-start.1 = (s32[8,128]{1,0:T(8,128)S(1)}, s32[8,128]{1,0:T(8,128)S(1)}, u32[]{:S(2)}, u32[]{:S(2)}) collective-permute-start(s32[8,128]{1,0:T(8,128)S(1)} %broadcast_in_dim.38), channel_id=1, source_target_pairs={{0,96},{16,112},{32,0},{48,16},{64,32},{80,48},{96,64},{112,80},{1... | collective-permute-start | bytes 12296 | tf_op jit(solution)/shard_map/ppermute | solution.py:230
  33.7 4.7 %collective-permute-start = (s32[8,128]{1,0:T(8,128)S(1)}, s32[8,128]{1,0:T(8,128)S(1)}, u32[]{:S(2)}, u32[]{:S(2)}) collective-permute-start(s32[8,128]{1,0:T(8,128)S(1)} %broadcast_in_dim.38), channel_id=1, source_target_pairs={{0,112},{16,0},{32,16},{48,32},{64,48},{80,64},{96,80},{112,96},{1... | collective-permute-start | bytes 12296 | tf_op jit(solution)/shard_map/ppermute | solution.py:230
  49.4 12.5 %collective-permute-start.8 = (bf16[32,256]{1,0:T(8,128)(2,1)S(1)}, bf16[32,256]{1,0:T(8,128)(2,1)S(1)}, u32[]{:S(2)}, u32[]{:S(2)}) collective-permute-start(bf16[32,256]{1,0:T(8,128)(2,1)S(1)} %get-tuple-element.6), channel_id=1, source_target_pairs={{16,0},{32,16},{48,32},{64,48},{80,64},{96,80},{112,96},{17,1},{33... | collective-permute-start | bytes 49160 | tf_op jit(solution)/shard_map/ppermute | solution.py:242
  50.7 10.0 %collective-permute-start.7 = (bf16[32,256]{1,0:T(8,128)(2,1)S(1)}, bf16[32,256]{1,0:T(8,128)(2,1)S(1)}, u32[]{:S(2)}, u32[]{:S(2)}) collective-permute-start(bf16[32,256]{1,0:T(8,128)(2,1)S(1)} %get-tuple-element.7), channel_id=1, source_target_pairs={{0,16},{16,32},{32,48},{48,64},{64,80},{80,96},{96,112},{1,17},{17... | collective-permute-start | bytes 49160 | tf_op jit(solution)/shard_map/ppermute | solution.py:241
  61.7 16.0 %copy-start.2 = (s32[1,8]{1,0:T(1,128)S(1)}, s32[1,8]{1,0:T(1,128)}, u32[]{:S(2)}) copy-start(s32[1,8]{1,0:T(1,128)} %param.10) | copy-start | bytes 100
  61.7 16.2 %copy-start.1 = (f32[1,1536,128]{2,1,0:T(8,128)S(1)}, f32[1,1536,128]{2,1,0:T(8,128)}, u32[]{:S(2)}) copy-start(f32[1,1536,128]{2,1,0:T(8,128)} %param.12) | copy-start | bytes 2359300
  76.8 289.4 %all-gather.5.cloned.1.call-start = ((), (), s32[]{:S(2)}) async-start(), calls=%async_computation.3 | async-start | bytes 6684672 | tf_op jit(solution)/shard_map/all_gather | solution.py:282
  170.3 133.9 %copy-start = (bf16[8,192,256]{2,1,0:T(8,128)(2,1)S(1)}, bf16[8,192,256]{2,1,0:T(8,128)(2,1)}, u32[]{:S(2)}) copy-start(bf16[8,192,256]{2,1,0:T(8,128)(2,1)} %all_to_all.31) | copy-start | bytes 2359300
Sparse Core Ops, SparseCore 0:
  76.9 93.3 all-gather.2
  304.4 61.7 all-gather.4
